TPU v7x, 32 devices: a whole 2x2x4 slice. The times are simulated.
32 devices in a mesh: space: 4 (over y, x), blk: 8 (over z, core).
Axes of the slice: x: 2, y: 2, z: 4, core: 2. Of those that a mesh axis runs over, the one named last changes fastest.
Arguments:
- density: bfloat16 [3072, 128, 128], P(('space', 'blk')), may hold values from -6 to 6
- bra_table: bfloat16 [3072, 128, 256], P(('space', 'blk')), may hold values from -0.5 to 0.5
- ket_table: bfloat16 [3072, 128, 256], P(('space', 'blk')), may hold values from -0.5 to 0.5
- box_of_block: int32 [3072], P(('space', 'blk')), may hold values from 0 to 63
- leaf_src: int32 [256, 27], P(('space', 'blk')), may hold values from 0 to 191
- leaf_type: int32 [256, 27], P(('space', 'blk')), may hold values from 0 to 15
- coarse_src: int32 [32, 27], P(('space', 'blk')), may hold values from 0 to 31
- coarse_type: int32 [32, 27], P(('space', 'blk')), may hold values from 0 to 15
- translation: float32 [16, 256, 256], replicated, may hold values from -0.375 to 0.375
- upward_translation_table: float32 [8, 256, 256], replicated, may hold values from -0.375 to 0.375
Outputs:
- coulomb: bfloat16 [3072, 128, 128], P(('space', 'blk'))
- box_locals: float32 [256, 256], P(('space', 'blk'))
All inputs are finite; a program needn't handle non-finite values.
Results may differ from a plain program's by a relative error of at most 0.0049.
Values sent between devices are 32-bit elements; how exact they have to be, the bound alone decides.
A program may use at most 128 MiB of HBM per device.

v0:
```python
import jax
import jax.numpy as jnp
from jax import lax
from jax.sharding import PartitionSpec as P


def padded(block, sides, width):
    for axis, dim in sides:
        count = lax.axis_size(axis)
        forward = [(i, i + 1) for i in range(count - 1)]
        backward = [(target, source) for source, target in forward]
        low = lax.ppermute(
            lax.slice_in_dim(block, block.shape[dim] - width, None, axis=dim), axis, forward
        )
        high = lax.ppermute(lax.slice_in_dim(block, 0, width, axis=dim), axis, backward)
        block = jnp.concatenate([low, block, high], axis=dim)
    return block


def shards(
    density,
    bra_table,
    ket_table,
    box_of_block,
    leaf_src,
    leaf_type,
    coarse_src,
    coarse_type,
    translation,
    upward_translation_table,
):
    top_level_index = lax.Precision.HIGHEST
    n_blk = lax.axis_size("blk")
    box_dom = 8 * n_blk
    n_types = translation.shape[0]
    inner = jnp.einsum("bmn,bmk->bnk", density, bra_table, preferred_element_type=jnp.float32)
    moments = jnp.sum(inner * ket_table.astype(jnp.float32), axis=1)
    box_hot = (box_of_block[:, None] == jnp.arange(box_dom, dtype=jnp.int32)[None, :]).astype(
        jnp.float32
    )
    partial_moments = lax.dot_general(
        box_hot, moments, (((0,), (0,)), ((), ())), precision=top_level_index
    )
    held_boxes = lax.psum_scatter(partial_moments, "blk", scatter_dimension=0, tiled=True)
    domain = lax.all_gather(held_boxes, "blk", axis=0, tiled=True)
    window = padded(domain, (("space", 0),), box_dom)
    self_parent_index = jnp.einsum(
        "oe,ode->d", held_boxes, upward_translation_table, precision=top_level_index
    )[None, :]
    all_parents = lax.all_gather(self_parent_index, ("space", "blk"), axis=0, tiled=True)
    src_hot = (leaf_src[..., None] == jnp.arange(3 * box_dom, dtype=jnp.int32)).astype(jnp.float32)
    type_hot = (leaf_type[..., None] == jnp.arange(n_types, dtype=jnp.int32)).astype(jnp.float32)
    counts = jnp.einsum("blt,blj->btj", type_hot, src_hot, precision=top_level_index)
    gathered = jnp.einsum("btj,jk->btk", counts, window, precision=top_level_index)
    leaf_far = jnp.einsum("btk,tlk->bl", gathered, translation, precision=top_level_index)
    n_parents = all_parents.shape[0]
    csrc_hot = (coarse_src[..., None] == jnp.arange(n_parents, dtype=jnp.int32)).astype(jnp.float32)
    ctype_hot = (coarse_type[..., None] == jnp.arange(n_types, dtype=jnp.int32)).astype(jnp.float32)
    ccounts = jnp.einsum("pet,peq->ptq", ctype_hot, csrc_hot, precision=top_level_index)
    cgathered = jnp.einsum("ptq,qk->ptk", ccounts, all_parents, precision=top_level_index)
    parent_local_expansion = jnp.einsum(
        "ptk,tlk->pl", cgathered, translation, precision=top_level_index
    )
    downward_sent = jnp.einsum(
        "d,uds->us", parent_local_expansion[0], upward_translation_table, precision=top_level_index
    )
    box_locals = leaf_far + downward_sent
    domain_local = lax.all_gather(box_locals, "blk", axis=0, tiled=True)
    block_locals = jnp.dot(box_hot, domain_local, precision=top_level_index)
    scaled = (bra_table.astype(jnp.float32) * block_locals[:, None, :]).astype(jnp.bfloat16)
    coulomb = jnp.einsum(
        "bmk,bnk->bmn", scaled, ket_table, preferred_element_type=jnp.float32
    ).astype(jnp.bfloat16)
    return (coulomb, box_locals)


def solution(mesh):
    placed = (
        P(("space", "blk"), None, None),
        P(("space", "blk"), None, None),
        P(("space", "blk"), None, None),
        P(("space", "blk")),
        P(("space", "blk"), None),
        P(("space", "blk"), None),
        P(("space", "blk"), None),
        P(("space", "blk"), None),
        P(),
        P(),
    )
    return jax.shard_map(
        shards,
        mesh=mesh,
        in_specs=placed,
        out_specs=(P(("space", "blk"), None, None), P(("space", "blk"), None)),
        check_vma=False,
    )
```

profile of v0, /device:TPU:0, one launch (start us, length us, event | category | flops | bytes accessed | tf_op | source)
XLA Modules:
  0.0 149.5 jit_solution(15269918359767577022)
XLA Ops:
  7.2 0.0 copy-start
  7.2 0.0 reduce-scatter.2.cloned.1.call-start
  7.3 1.8 %copy-done = bf16[96,128,128]{2,1,0:T(8,128)(2,1)S(1)} copy-done((bf16[96,128,128]{2,1,0:T(8,128)(2,1)S(1)}, bf16[96,128,128]{2,1,0:T(8,128)(2,1)}, u32[]{:S(2)}) %copy-start) | copy-done | bytes 3145752
  9.1 6.8 %multiply_reduce_fusion = f32[96,256]{1,0:T(8,128)S(1)} fusion(bf16[96,128,256]{2,1,0:T(8,128)(2,1)} %param.12, bf16[96,128,128]{2,1,0:T(8,128)(2,1)S(1)} %copy-done, bf16[96,128,256]{2,1,0:T(8,128)(2,1)} %param.11), kind=kOutput, calls=%fused_computation.1 | convolution fusion | flops 814718976 | bytes 15826944 | tf_op jit(solution)/shard_map/bmn,bmk->bnk/dot_general | solution.py:36
  15.9 0.9 fusion.13
  16.8 0.0 reduce-scatter.2.cloned.1.call-update
  16.9 0.2 fusion.4
  17.1 0.0 copy-done.8
  17.1 0.2 fusion.21
  17.3 32.5 %reduce-scatter.2.cloned.1.call-done = f32[8,256]{1,0:T(8,128)} async-done(((f32[64,256]{1,0:T(8,128)}), f32[8,256]{1,0:T(8,128)}) %reduce-scatter.2.cloned.1.call-update) | async-done | bytes 8208 | tf_op jit(solution)/shard_map/reduce_scatter | solution.py:44
  49.8 14.3 %all_gather.9 = f32[64,256]{1,0:T(8,128)S(1)} all-gather(f32[8,256]{1,0:T(8,128)} %reduce-scatter.2.cloned.1.call-done), channel_id=1, replica_groups=mesh['space'=4,'blk'=8] {'blk'}, dimensions={0}, use_global_device_ids=true | all-gather | bytes 73728 | tf_op jit(solution)/shard_map/all_gather | solution.py:45
  64.1 1.3 collective-permute-start.1
  65.4 4.5 %collective-permute-start = (f32[64,256]{1,0:T(8,128)S(1)}, f32[64,256]{1,0:T(8,128)S(1)}, u32[]{:S(2)}, u32[]{:S(2)}) collective-permute-start(f32[64,256]{1,0:T(8,128)S(1)} %all_gather.9), channel_id=1, source_target_pairs={{0,8},{8,16},{16,24},{1,9},{9,17},{17,25},{2,10},{10,18},{18,26},{... | collective-permute-start | bytes 196616 | tf_op jit(solution)/shard_map/ppermute | solution.py:12
  70.0 3.3 %convolution_bitcast_fusion.3 = f32[1,1,256]{2,1,0:T(1,128)S(1)} fusion(f32[8,256,256]{2,1,0:T(8,128)} %param.19, f32[8,256,1]{1,0,2:T(8,128)} %bitcast.43), kind=kOutput, calls=%fused_computation.9 | convolution fusion | flops 6291456 | bytes 2106368 | tf_op jit(solution)/shard_map/oe,ode->d/dot_general | solution.py:47
  73.3 36.6 %all-gather.1 = f32[32,1,256]{2,1,0:T(1,128)S(1)} all-gather(f32[1,1,256]{2,1,0:T(1,128)S(1)} %convolution_bitcast_fusion.3), channel_id=2, replica_groups=mesh['space'=4,'blk'=8] {'space','blk'}, dimensions={0}, use_global_device_ids=true | all-gather | bytes 33792 | tf_op jit(solution)/shard_map/all_gather | solution.py:50
  109.9 0.1 convolution_bitcast_fusion
  110.0 5.5 %convolution_bitcast_fusion.2 = f32[256,1,1]{0,1,2:T(1,128)S(1)} fusion(f32[16,256,256]{2,1,0:T(8,128)} %param.18, f32[16,256,1]{1,0,2:T(8,128)S(1)} %convolution_bitcast_fusion), kind=kOutput, calls=%fused_computation.8 | convolution fusion | flops 12582912 | bytes 4211712 | tf_op jit(solution)/shard_map/ptk,tlk->pl/dot_general | solution.py:61
  115.5 1.1 fusion.29
  116.7 0.0 collective-permute-done
  116.7 0.3 fusion.5
  117.0 3.3 %fusion.3 = f32[8,256]{1,0:T(8,128)S(1)} fusion(f32[8,16,256]{2,0,1:T(8,128)S(1)} %fusion.5, f32[16,256,256]{2,1,0:T(8,128)S(1)} %copy-done.1, f32[1,8,256]{2,0,1:T(1,128)S(1)} %fusion.29), kind=kOutput, calls=%fused_computation.7 | convolution fusion | flops 100665344 | bytes 4341760 | tf_op jit(solution)/shard_map/btk,tlk->bl/dot_general | solution.py:55
  120.3 14.0 %all_gather.11 = f32[64,256]{1,0:T(8,128)S(1)} all-gather(f32[8,256]{1,0:T(8,128)S(1)} %fusion.3), channel_id=1, replica_groups=mesh['space'=4,'blk'=8] {'blk'}, dimensions={0}, use_global_device_ids=true | all-gather | bytes 73728 | tf_op jit(solution)/shard_map/all_gather | solution.py:68
  134.3 0.2 fusion.12
  134.6 8.1 %fusion.2 = bf16[96,128,128]{2,1,0:T(8,128)(2,1)} fusion(bf16[96,128,256]{2,1,0:T(8,128)(2,1)} %param.12, bf16[96,128,256]{2,1,0:T(8,128)(2,1)} %param.11, f32[96,256]{1,0:T(8,128)S(1)} %fusion.12), kind=kOutput, calls=%fused_computation.4 | convolution fusion | flops 816316416 | bytes 15826944 | tf_op jit(solution)/shard_map/bmk,bnk->bmn/dot_general | solution.py:71
  (16 shorter events, 0.0 us)
Async XLA Ops:
  7.2 1.9 %copy-start = (bf16[96,128,128]{2,1,0:T(8,128)(2,1)S(1)}, bf16[96,128,128]{2,1,0:T(8,128)(2,1)}, u32[]{:S(2)}) copy-start(bf16[96,128,128]{2,1,0:T(8,128)(2,1)} %param.10) | copy-start | bytes 9437188
  7.2 8.7 %copy-start.6 = (s32[96]{0:T(128)S(1)}, s32[96]{0:T(128)}, u32[]{:S(2)}) copy-start(s32[96]{0:T(128)} %param.13) | copy-start | bytes 1156
  7.2 9.7 %copy-start.5 = (s32[8,27]{1,0:T(8,128)S(1)}, s32[8,27]{1,0:T(8,128)}, u32[]{:S(2)}) copy-start(s32[8,27]{1,0:T(8,128)} %param.15) | copy-start | bytes 2596
  7.2 9.7 %copy-start.4 = (s32[8,27]{1,0:T(8,128)S(1)}, s32[8,27]{1,0:T(8,128)}, u32[]{:S(2)}) copy-start(s32[8,27]{1,0:T(8,128)} %param.14) | copy-start | bytes 2596
  7.2 9.9 %copy-start.8 = (s32[1,27]{1,0:T(1,128)S(1)}, s32[1,27]{1,0:T(1,128)}, u32[]{:S(2)}) copy-start(s32[1,27]{1,0:T(1,128)} %param.17) | copy-start | bytes 328
  7.2 9.9 %copy-start.7 = (s32[1,27]{1,0:T(1,128)S(1)}, s32[1,27]{1,0:T(1,128)}, u32[]{:S(2)}) copy-start(s32[1,27]{1,0:T(1,128)} %param.16) | copy-start | bytes 328
  7.2 42.6 %reduce-scatter.2.cloned.1.call-start = ((), (), s32[]{:S(2)}) async-start(), calls=%async_computation.1 | async-start | bytes 73728 | tf_op jit(solution)/shard_map/reduce_scatter | solution.py:44
  49.8 65.8 %copy-start.2 = (f32[8,256,256]{2,1,0:T(8,128)S(1)}, f32[8,256,256]{2,1,0:T(8,128)}, u32[]{:S(2)}) copy-start(f32[8,256,256]{2,1,0:T(8,128)} %param.19) | copy-start | bytes 6291460
  49.8 67.2 %copy-start.1 = (f32[16,256,256]{2,1,0:T(8,128)S(1)}, f32[16,256,256]{2,1,0:T(8,128)}, u32[]{:S(2)}) copy-start(f32[16,256,256]{2,1,0:T(8,128)} %param.18) | copy-start | bytes 12582916
  64.1 52.6 %collective-permute-start.1 = (f32[64,256]{1,0:T(8,128)S(1)}, f32[64,256]{1,0:T(8,128)S(1)}, u32[]{:S(2)}, u32[]{:S(2)}) collective-permute-start(f32[64,256]{1,0:T(8,128)S(1)} %all_gather.9), channel_id=1, source_target_pairs={{8,0},{16,8},{24,16},{9,1},{17,9},{25,17},{10,2},{18,10},{26,18},{... | collective-permute-start | bytes 196616 | tf_op jit(solution)/shard_map/ppermute | solution.py:15
  65.4 51.3 %collective-permute-start = (f32[64,256]{1,0:T(8,128)S(1)}, f32[64,256]{1,0:T(8,128)S(1)}, u32[]{:S(2)}, u32[]{:S(2)}) collective-permute-start(f32[64,256]{1,0:T(8,128)S(1)} %all_gather.9), channel_id=1, source_target_pairs={{0,8},{8,16},{16,24},{1,9},{9,17},{17,25},{2,10},{10,18},{18,26},{... | collective-permute-start | bytes 196616 | tf_op jit(solution)/shard_map/ppermute | solution.py:12
  120.3 22.3 %copy-start.3 = (f32[8,256]{1,0:T(8,128)}, f32[8,256]{1,0:T(8,128)S(1)}, u32[]{:S(2)}) copy-start(f32[8,256]{1,0:T(8,128)S(1)} %fusion.3) | copy-start | bytes 24580
Sparse Core Ops, SparseCore 0:
  17.0 32.7 reduce-scatter.1
where the time goes:
time: 150 us
  blocking collectives  64.9 us (43%)
  waiting for transfers between devices  32.5 us (22%)
  matrix products  30.3 us (20%)
  between operations  14.2 us (9%)
  starting transfers between devices  5.87 us (4%)
  local copies, waits for them, and re-layouts  1.83 us (1%)
    all_gather x1, blocking collectives, shards(): lax.all_gather(self_parent_index, ('space', 'blk'), axis=0, tiled=True)  36.6 us
    reduce_scatter x1, waiting for transfers between devices, shards(): lax.psum_scatter(partial_moments, 'blk', scatter_dimension=0, tiled=True)  32.5 us
    all_gather x1, blocking collectives, shards(): domain = lax.all_gather(held_boxes, 'blk', axis=0, tiled=True)  14.3 us
    all_gather x1, blocking collectives, shards(): domain_local = lax.all_gather(box_locals, 'blk', axis=0, tiled=True)  14 us
    dot_general x1, matrix products, shards(): jnp.einsum('bmk,bnk->bmn', scaled, ket_table, preferred_element_type=jnp....  8.08 us
    dot_general x1, matrix products, shards(): jnp.einsum('bmn,bmk->bnk', density, bra_table, preferred_element_type=jnp...  6.82 us
    dot_general x1, matrix products, shards(): jnp.einsum('ptk,tlk->pl', cgathered, translation, precision=top_level_index)  5.55 us
    ppermute x1, starting transfers between devices, padded(): lax.ppermute(lax.slice_in_dim(block, block.shape[dim] - width, None, axis...  4.55 us
  transfers between devices with their start and end apart: 3, of which 1 were waited for; matrix products, arithmetic and copies ran while one was open for 7% of the time, Pallas kernels for 0%

commit v1 on v0

v1 whole, which is shorter than its diff:
```python
import functools

import jax
import jax.numpy as jnp
from jax import lax
from jax.experimental import pallas as pl
from jax.experimental.pallas import tpu as pltpu
from jax.sharding import PartitionSpec as P

MESH = pl.DeviceIdType.MESH
F32 = jnp.float32
BF16 = jnp.bfloat16
GROUP = 8
KEY = 1024


def dot(a, b, dims):
    return lax.dot_general(a, b, (dims, ((), ())), preferred_element_type=F32)


NN = ((1,), (0,))
NT = ((1,), (1,))
TN = ((0,), (0,))


def halves(x):
    high = x.astype(BF16)
    return high, (x - high.astype(F32)).astype(BF16)


def one_hot_dot(hot, x, dims):
    high, low = halves(x)
    return dot(hot, high, dims) + dot(hot, low, dims)


def split_dot(x, w, dims):
    rows = x.shape[0]
    x_high, x_low = halves(x)
    w_high, w_low = halves(w)
    both = dot(jnp.concatenate([x_high, x_low], axis=0), w_high, dims)
    return both[:rows] + both[rows:] + dot(x_high, w_low, dims)


def count_hot(keys, width):
    rows, entries = keys.shape
    lane = lax.broadcasted_iota(jnp.int32, (rows, width), 1)
    total = jnp.zeros((rows, width), F32)
    for e in range(entries):
        total += jnp.where(lane == keys[:, e : e + 1], 1.0, 0.0)
    return total


def build(
    n_space,
    n_blk,
    n_types,
    den_hbm, bra_hbm, ket_hbm, box_ref, lsrc_ref, ltype_ref, csrc_ref, ctype_ref, t_hbm, u_hbm,
    out_ref, mine_ref,
    den, bra, ket, t_ref, u_ref, mom, part, sib, lists, c_leaf, c_top, x_ref, v_high, v_low, v_top,
    leaf_out, top_out, leaf_in, top_in, dom, rows_ref, acc, kids,
    load_sem, table_sem, list_send, list_recv, sib_send, sib_recv,
    leaf_send, leaf_recv, top_send, top_recv, dom_send, dom_recv,
):
    s = lax.axis_index("space")
    j = lax.axis_index("blk")
    core = lax.rem(j, 2)
    z = j // 2
    other = j + 1 - 2 * core
    nz = n_blk // 2
    box_dom = 8 * n_blk
    top_dom = n_blk
    n_blocks = den.shape[0]
    chunks = n_blocks // GROUP
    entries = lsrc_ref.shape[1]
    me = s * nz + z
    groups = n_space * nz

    barrier = pltpu.get_barrier_semaphore()
    for o in range(1, groups):
        g = lax.rem(me + o, groups)
        pl.semaphore_signal(
            barrier, inc=1, device_id=(g // nz, lax.rem(g, nz) * 2 + core), device_id_type=MESH
        )
    for k in range(nz):
        pl.semaphore_signal(barrier, inc=1, device_id=(s, k * 2 + 1 - core), device_id_type=MESH)

    def loads(i):
        at = pl.ds(i * GROUP, GROUP)
        return [
            pltpu.make_async_copy(src.at[at], dst.at[at], load_sem.at[k, i])
            for k, (src, dst) in enumerate(((den_hbm, den), (ket_hbm, ket), (bra_hbm, bra)))
        ]

    def start_loads(i, carry):
        for copy in loads(i):
            copy.start()
        return carry

    lax.fori_loop(0, chunks, start_loads, 0)
    u_copy = pltpu.make_async_copy(u_hbm, u_ref, table_sem.at[0])
    t_copy = pltpu.make_async_copy(t_hbm, t_ref, table_sem.at[1])
    u_copy.start()
    t_copy.start()

    lists[pl.ds(me * 16, 8), 0:entries] = ltype_ref[...] * KEY + lsrc_ref[...]
    lists[pl.ds(me * 16 + 8, 1), 0:entries] = ctype_ref[...] * KEY + csrc_ref[...]
    pl.semaphore_wait(barrier, groups - 1 + nz)

    def list_copy(o):
        g = lax.rem(me + o, groups)
        at = pl.ds(me * 16, 16)
        return pltpu.make_async_remote_copy(
            src_ref=lists.at[at],
            dst_ref=lists.at[at],
            send_sem=list_send.at[o],
            recv_sem=list_recv.at[me],
            device_id=(g // nz, lax.rem(g, nz) * 2 + core),
            device_id_type=MESH,
        )

    def list_arrival(o):
        g = lax.rem(me + o, groups)
        at = pl.ds(g * 16, 16)
        return pltpu.make_async_remote_copy(
            src_ref=lists.at[at],
            dst_ref=lists.at[at],
            send_sem=list_send.at[o],
            recv_sem=list_recv.at[g],
            device_id=(g // nz, lax.rem(g, nz) * 2 + core),
            device_id_type=MESH,
        )

    for o in range(1, groups):
        list_copy(o).start()

    def moments(i, carry):
        for copy in loads(i):
            copy.wait()
        rows = []
        for u in range(GROUP):
            b = i * GROUP + u
            inner = dot(den[b], ket[b], NN)
            rows.append(jnp.sum(inner * bra[b].astype(F32), axis=0, keepdims=True))
        mom[pl.ds(i * GROUP, GROUP), :] = jnp.concatenate(rows, axis=0)
        return carry

    lax.fori_loop(0, chunks, moments, 0)
    hot = jnp.where(
        lax.broadcasted_iota(jnp.int32, (box_dom, n_blocks), 0) == box_ref[...], 1.0, 0.0
    ).astype(BF16)
    part[...] = one_hot_dot(hot, mom[...], NN)

    sib_copy = pltpu.make_async_remote_copy(
        src_ref=part,
        dst_ref=sib,
        send_sem=sib_send,
        recv_sem=sib_recv,
        device_id=(s, other),
        device_id_type=MESH,
    )
    sib_copy.start()

    for o in range(1, groups):
        list_arrival(o).wait_recv()
    for w in range(3):
        sender_at = 2 - w
        target = jnp.clip(s + w - 1, 0, n_space - 1)
        for k in range(nz):
            packed = lists[pl.ds((target * nz + k) * 16, 8), 0:entries]
            kind = lax.shift_right_logical(packed, 10)
            place = (packed & (KEY - 1)) - sender_at * box_dom
            keys = jnp.where((place >= 0) & (place < box_dom), kind * box_dom + place, -1)
            c_leaf[pl.ds((w * nz + k) * 8, 8), :] = count_hot(keys, n_types * box_dom)
    packed = lists[pl.ds(8, groups, stride=16), :]
    kind = lax.shift_right_logical(packed, 10)
    place = (packed & (KEY - 1)) - s * top_dom
    keys = jnp.where((place >= 0) & (place < top_dom), kind * top_dom + place, -1)
    c_top[...] = count_hot(keys[:, 0:entries], n_types * top_dom)

    u_copy.wait()
    t_copy.wait()
    sib_copy.wait()
    own = part[...] + sib[...]
    x_ref[0:box_dom, :] = own
    kids[0:box_dom, :] = own[:, 0:128]
    kids[box_dom:, :] = own[:, 128:]
    x_ref[box_dom:, :] = jnp.zeros((x_ref.shape[0] - box_dom, x_ref.shape[1]), F32)

    tops = jnp.zeros((top_dom, x_ref.shape[1]), F32)
    for c in range(8):
        child = jnp.concatenate(
            [kids[pl.ds(h * box_dom + c, top_dom, stride=8), :] for h in range(2)], axis=1
        )
        c_high, c_low = halves(child)
        stack = jnp.concatenate([c_high.astype(F32), c_low.astype(F32)], axis=0).astype(BF16)
        u_high, u_low = halves(u_ref[c])
        both = dot(stack, u_high, NT)
        extra = dot(stack, u_low, NT)
        tops += both[:top_dom] + both[top_dom:] + extra[:top_dom]
    x_ref[box_dom : box_dom + top_dom, :] = tops

    x = x_ref[...]
    x_high, x_low = halves(x)
    x_rows = x.shape[0]
    stack = jnp.concatenate([x_high, x_low], axis=0)
    for t in range(n_types):
        t_high, t_low = halves(t_ref[t])
        both = dot(stack, t_high, NT)
        v = both[:x_rows] + both[x_rows:] + dot(x_high, t_low, NT)
        high, low = halves(v[:box_dom])
        v_high[t * box_dom : (t + 1) * box_dom, :] = high
        v_low[t * box_dom : (t + 1) * box_dom, :] = low
        v_top[t * top_dom : (t + 1) * top_dom, :] = v[box_dom : box_dom + top_dom]

    sent_top = one_hot_dot(c_top[...].astype(BF16), v_top[...], NN)
    for g in range(groups):
        top_out[g] = sent_top[g : g + 1, :]

    def top_copy(o, source):
        g = lax.rem(me + o, groups)
        return pltpu.make_async_remote_copy(
            src_ref=top_out.at[g],
            dst_ref=top_in.at[source],
            send_sem=top_send.at[o],
            recv_sem=top_recv.at[source],
            device_id=(g // nz, lax.rem(g, nz) * 2 + core),
            device_id_type=MESH,
        )

    for o in range(1, groups):
        top_copy(o, me).start()
    top_in[pl.ds(me, 1)] = top_out[pl.ds(me, 1)]

    hot_leaf = c_leaf[...].astype(BF16)
    sent = dot(hot_leaf, v_high[...], NN) + dot(hot_leaf, v_low[...], NN)
    leaf_out[...] = sent.reshape(3 * nz, 8, sent.shape[1])

    def leaf_copy(w, o, source):
        k = lax.rem(z + o, nz)
        n = w * nz + o
        return pltpu.make_async_remote_copy(
            src_ref=leaf_out.at[w * nz + k],
            dst_ref=leaf_in.at[source],
            send_sem=leaf_send.at[n],
            recv_sem=leaf_recv.at[source],
            device_id=(jnp.clip(s + w - 1, 0, n_space - 1), k * 2 + core),
            device_id_type=MESH,
        )

    has = (s > 0, None, s < n_space - 1)
    for w in (0, 2):
        @pl.when(has[w])
        def _():
            for o in range(nz):
                leaf_copy(w, o, (2 - w) * nz + z).start()
    for o in range(1, nz):
        leaf_copy(1, o, nz + z).start()

    total = jnp.zeros((1, x_ref.shape[1]), F32)
    for o in range(1, groups):
        top_copy(o, lax.rem(me + o, groups)).wait_recv()
    for g in range(groups):
        total += top_in[g]
    total_high, total_low = halves(total)
    stack = jnp.concatenate(
        [total_high.astype(F32), total_low.astype(F32), jnp.zeros((14, total.shape[1]), F32)], axis=0
    ).astype(BF16)
    down = []
    for c in range(8):
        u_high, u_low = halves(u_ref[c])
        both = dot(stack, u_high, NN)
        extra = dot(stack, u_low, NN)
        down.append(both[0:1] + both[1:2] + extra[0:1])
    acc[...] = jnp.concatenate(down, axis=0) + leaf_out[pl.ds(nz + z, 1)][0]
    for o in range(1, nz):
        source = nz + lax.rem(z + o, nz)
        leaf_copy(1, o, source).wait_recv()
        acc[...] += leaf_in[pl.ds(source, 1)][0]
    for w in (0, 2):
        @pl.when(has[w])
        def _():
            for o in range(nz):
                source = w * nz + lax.rem(z + o, nz)
                leaf_copy(w, o, source).wait_recv()
                acc[...] += leaf_in[pl.ds(source, 1)][0]
    mine_ref[...] = acc[...]
    here = pl.ds(j * 8, 8)
    dom[here, :] = acc[...]

    def dom_copy(o, source):
        at = pl.ds(source * 8, 8)
        return pltpu.make_async_remote_copy(
            src_ref=dom.at[at],
            dst_ref=dom.at[at],
            send_sem=dom_send.at[o],
            recv_sem=dom_recv.at[source],
            device_id=(s, lax.rem(j + o, n_blk)),
            device_id_type=MESH,
        )

    for o in range(1, n_blk):
        dom_copy(o, j).start()
    for o in range(1, n_blk):
        dom_copy(o, lax.rem(j + o, n_blk)).wait_recv()

    rows_ref[...] = one_hot_dot(hot, dom[...], TN)

    def contract(i, carry):
        local = rows_ref[pl.ds(i * GROUP, GROUP), :]
        for u in range(GROUP):
            b = i * GROUP + u
            scaled = (bra[b].astype(F32) * local[u : u + 1, :]).astype(BF16)
            out_ref[b] = dot(scaled, ket[b], NT).astype(BF16)
        return carry

    lax.fori_loop(0, chunks, contract, 0)

    for o in range(1, groups):
        list_copy(o).wait_send()
        top_copy(o, me).wait_send()
    for w in (0, 2):
        @pl.when(has[w])
        def _():
            for o in range(nz):
                leaf_copy(w, o, (2 - w) * nz + z).wait_send()
    for o in range(1, nz):
        leaf_copy(1, o, nz + z).wait_send()
    for o in range(1, n_blk):
        dom_copy(o, j).wait_send()


def shards(
    density,
    bra_table,
    ket_table,
    box_of_block,
    leaf_src,
    leaf_type,
    coarse_src,
    coarse_type,
    translation,
    upward_translation_table,
):
    n_space = lax.axis_size("space")
    n_blk = lax.axis_size("blk")
    nz = n_blk // 2
    groups = n_space * nz
    n_blocks, side, coeffs = bra_table.shape
    n_types = translation.shape[0]
    box_dom = 8 * n_blk
    top_dom = n_blk
    chunks = n_blocks // GROUP
    x_rows = -(-(box_dom + top_dom) // 16) * 16
    whole = pl.BlockSpec(memory_space=pltpu.VMEM)
    far = pl.BlockSpec(memory_space=pl.ANY)
    dma = pltpu.SemaphoreType.DMA
    coulomb, box_locals = pl.pallas_call(
        functools.partial(build, n_space, n_blk, n_types),
        out_shape=(
            jax.ShapeDtypeStruct((n_blocks, side, side), BF16),
            jax.ShapeDtypeStruct((8, coeffs), F32),
        ),
        in_specs=[far, far, far, whole, whole, whole, whole, whole, far, far],
        out_specs=(whole, whole),
        scratch_shapes=[
            pltpu.VMEM(density.shape, BF16),
            pltpu.VMEM(bra_table.shape, BF16),
            pltpu.VMEM(ket_table.shape, BF16),
            pltpu.VMEM(translation.shape, F32),
            pltpu.VMEM(upward_translation_table.shape, F32),
            pltpu.VMEM((n_blocks, coeffs), F32),
            pltpu.VMEM((box_dom, coeffs), F32),
            pltpu.VMEM((box_dom, coeffs), F32),
            pltpu.VMEM((groups * 16, 128), jnp.int32),
            pltpu.VMEM((3 * nz * 8, n_types * box_dom), F32),
            pltpu.VMEM((groups, n_types * top_dom), F32),
            pltpu.VMEM((x_rows, coeffs), F32),
            pltpu.VMEM((n_types * box_dom, coeffs), BF16),
            pltpu.VMEM((n_types * box_dom, coeffs), BF16),
            pltpu.VMEM((n_types * top_dom, coeffs), F32),
            pltpu.VMEM((3 * nz, 8, coeffs), F32),
            pltpu.VMEM((groups, 1, coeffs), F32),
            pltpu.VMEM((3 * nz, 8, coeffs), F32),
            pltpu.VMEM((groups, 1, coeffs), F32),
            pltpu.VMEM((box_dom, coeffs), F32),
            pltpu.VMEM((n_blocks, coeffs), F32),
            pltpu.VMEM((8, coeffs), F32),
            pltpu.VMEM((2 * box_dom, coeffs // 2), F32),
            dma((3, chunks)),
            dma((2,)),
            dma((groups,)),
            dma((groups,)),
            dma,
            dma,
            dma((3 * nz,)),
            dma((3 * nz,)),
            dma((groups,)),
            dma((groups,)),
            dma((n_blk,)),
            dma((n_blk,)),
        ],
        compiler_params=pltpu.CompilerParams(
            collective_id=0, has_side_effects=True, vmem_limit_bytes=48 * 1024 * 1024
        ),
        cost_estimate=pl.CostEstimate(
            flops=4 * n_blocks * side * side * coeffs,
            bytes_accessed=30_000_000,
            transcendentals=0,
        ),
    )(
        density,
        bra_table,
        ket_table,
        box_of_block[None, :],
        leaf_src,
        leaf_type,
        coarse_src,
        coarse_type,
        translation,
        upward_translation_table,
    )
    return coulomb, box_locals


def solution(mesh):
    placed = (
        P(("space", "blk"), None, None),
        P(("space", "blk"), None, None),
        P(("space", "blk"), None, None),
        P(("space", "blk")),
        P(("space", "blk"), None),
        P(("space", "blk"), None),
        P(("space", "blk"), None),
        P(("space", "blk"), None),
        P(),
        P(),
    )
    return jax.shard_map(
        shards,
        mesh=mesh,
        in_specs=placed,
        out_specs=(P(("space", "blk"), None, None), P(("space", "blk"), None)),
        check_vma=False,
    )
```

time: 150 us -> 36.8 us (0.25)
  blocking collectives: 64.9 us -> 0 us
  waiting for transfers between devices: 32.5 us -> 0 us
  matrix products: 30.3 us -> 0 us
  Pallas kernels: 0 us -> 28.7 us
  between operations: 14.2 us -> 0.66 us
  starting transfers between devices: 5.87 us -> 0 us
  local copies, waits for them, and re-layouts: 1.83 us -> 7.19 us
    all_gather x3 -> x0, blocking collectives: 64.9 us -> none  [the longest x1 36.6 us: shards(): lax.all_gather(self_parent_index, ('space', 'blk'), axis=0, tiled=True)]
    reduce_scatter x1 -> x0, waiting for transfers between devices: 32.5 us -> none  [shards(): lax.psum_scatter(partial_moments, 'blk', scatter_dimension=0, tiled=True)]
    dot_general x12 -> x0, matrix products: 30.3 us -> none  [the longest x1 8.08 us: shards(): jnp.einsum('bmk,bnk->bmn', scaled, ket_table, preferred_element_type=jnp....]
    pallas_call x0 -> x1, Pallas kernels: none -> 28.7 us  [shards(): pl.pallas_call(functools.partial(build, n_space, n_blk, n_types), out_sha...]
    ppermute x2 -> x0, starting transfers between devices: 5.83 us -> none  [the longest x1 4.55 us: padded(): lax.ppermute(lax.slice_in_dim(block, block.shape[dim] - width, None, axis...]
    unnamed x18 -> x14, local copies, waits for them, and re-layouts: 1.83 us -> 7.19 us
  transfers between devices with their start and end apart: 3 -> 0, of which waited for: 1 -> 0; matrix products, arithmetic and copies ran while one was open for 7% -> 0% of each run, Pallas kernels for 0% -> 0%
where the time goes in v1:
time: 36.8 us; the launch traced here: 36.6 us
  Pallas kernels  28.7 us (78%)
  local copies, waits for them, and re-layouts  7.19 us (20%)
  between operations  0.66 us (2%)
    pallas_call x1, Pallas kernels, shards(): pl.pallas_call(functools.partial(build, n_space, n_blk, n_types), out_sha...  28.7 us
    unnamed x14, local copies, waits for them, and re-layouts  7.19 us

profile of v1, /device:TPU:0, one launch (start us, length us, event | category | flops | bytes accessed | tf_op | source)
XLA Modules:
  0.0 36.6 jit_solution(4684238995086828402)
XLA Ops:
  0.6 0.0 copy-start
  0.6 1.6 %copy-done = f32[8,256,256]{2,1,0:T(8,128)S(1)} copy-done((f32[8,256,256]{2,1,0:T(8,128)S(1)}, f32[8,256,256]{2,1,0:T(8,128)}, u32[]{:S(2)}) %copy-start) | copy-done | bytes 2097176
  2.2 0.0 copy-start.1
  2.2 0.7 %copy-done.1 = s32[8,27]{1,0:T(8,128)S(1)} copy-done((s32[8,27]{1,0:T(8,128)S(1)}, s32[8,27]{1,0:T(8,128)}, u32[]{:S(2)}) %copy-start.1) | copy-done | bytes 888
  2.9 0.0 copy-start.2
  2.9 0.7 %copy-done.2 = s32[8,27]{1,0:T(8,128)S(1)} copy-done((s32[8,27]{1,0:T(8,128)S(1)}, s32[8,27]{1,0:T(8,128)}, u32[]{:S(2)}) %copy-start.2) | copy-done | bytes 888
  3.6 0.0 copy-start.3
  3.6 0.7 %copy-done.3 = s32[96]{0:T(128)S(1)} copy-done((s32[96]{0:T(128)S(1)}, s32[96]{0:T(128)}, u32[]{:S(2)}) %copy-start.3) | copy-done | bytes 408
  4.3 0.0 copy-start.4
  4.3 0.7 %copy-done.4 = s32[1,27]{1,0:T(1,128)S(1)} copy-done((s32[1,27]{1,0:T(1,128)S(1)}, s32[1,27]{1,0:T(1,128)}, u32[]{:S(2)}) %copy-start.4) | copy-done | bytes 132
  4.9 0.0 copy-start.5
  4.9 0.7 %copy-done.5 = s32[1,27]{1,0:T(1,128)S(1)} copy-done((s32[1,27]{1,0:T(1,128)S(1)}, s32[1,27]{1,0:T(1,128)}, u32[]{:S(2)}) %copy-start.5) | copy-done | bytes 132
  5.6 28.7 %shard_map.113 = (bf16[96,128,128]{2,1,0:T(8,128)(2,1)S(1)}, f32[8,256]{1,0:T(8,128)S(1)}) custom-call(bf16[96,128,128]{2,1,0:T(8,128)(2,1)} %den_hbm.1, bf16[96,128,256]{2,1,0:T(8,128)(2,1)} %bra_hbm.1, bf16[96,128,256]{2,1,0:T(8,128)(2,1)} %ket_hbm.1, s32[1,96]{1,0:T(1,128)S(1)} %bitcast.1, s32[8,27]{1,0:T(8,128)S(1)} %copy-done.1, s32[8,27]{1,0:T(8,128)S(1)} %copy-done.2, ...), custom_call_target="tpu_custom_call" | custom-call | flops 1610612736 | bytes 30000000 | tf_op jit(solution)/shard_map/pallas_call | solution.py:357
  34.3 1.7 %copy.14 = bf16[96,128,128]{2,1,0:T(8,128)(2,1)} copy(bf16[96,128,128]{2,1,0:T(8,128)(2,1)S(1)} %get-tuple-element.4) | data formatting | bytes 6291456
  36.0 0.6 %copy.15 = f32[8,256]{1,0:T(8,128)} copy(f32[8,256]{1,0:T(8,128)S(1)} %get-tuple-element.5) | data formatting | bytes 16384
Async XLA Ops:
  0.6 1.6 %copy-start = (f32[8,256,256]{2,1,0:T(8,128)S(1)}, f32[8,256,256]{2,1,0:T(8,128)}, u32[]{:S(2)}) copy-start(f32[8,256,256]{2,1,0:T(8,128)} %u_hbm.1) | copy-start | bytes 6291460
  2.2 0.7 %copy-start.1 = (s32[8,27]{1,0:T(8,128)S(1)}, s32[8,27]{1,0:T(8,128)}, u32[]{:S(2)}) copy-start(s32[8,27]{1,0:T(8,128)} %lsrc_ref.1) | copy-start | bytes 2596
  2.9 0.7 %copy-start.2 = (s32[8,27]{1,0:T(8,128)S(1)}, s32[8,27]{1,0:T(8,128)}, u32[]{:S(2)}) copy-start(s32[8,27]{1,0:T(8,128)} %ltype_ref.1) | copy-start | bytes 2596
  3.6 0.7 %copy-start.3 = (s32[96]{0:T(128)S(1)}, s32[96]{0:T(128)}, u32[]{:S(2)}) copy-start(s32[96]{0:T(128)} %param.13) | copy-start | bytes 1156
  4.3 0.7 %copy-start.4 = (s32[1,27]{1,0:T(1,128)S(1)}, s32[1,27]{1,0:T(1,128)}, u32[]{:S(2)}) copy-start(s32[1,27]{1,0:T(1,128)} %csrc_ref.1) | copy-start | bytes 328
  4.9 0.7 %copy-start.5 = (s32[1,27]{1,0:T(1,128)S(1)}, s32[1,27]{1,0:T(1,128)}, u32[]{:S(2)}) copy-start(s32[1,27]{1,0:T(1,128)} %ctype_ref.1) | copy-start | bytes 328

commit v2 on v1

--- a/solution.py
+++ b/solution.py
@@ -31,14 +31,6 @@
 def one_hot_dot(hot, x, dims):
     high, low = halves(x)
     return dot(hot, high, dims) + dot(hot, low, dims)
-
-
-def split_dot(x, w, dims):
-    rows = x.shape[0]
-    x_high, x_low = halves(x)
-    w_high, w_low = halves(w)
-    both = dot(jnp.concatenate([x_high, x_low], axis=0), w_high, dims)
-    return both[:rows] + both[rows:] + dot(x_high, w_low, dims)
 
 
 def count_hot(keys, width):
@@ -54,11 +46,11 @@
     n_space,
     n_blk,
     n_types,
-    den_hbm, bra_hbm, ket_hbm, box_ref, lsrc_ref, ltype_ref, csrc_ref, ctype_ref, t_hbm, u_hbm,
-    out_ref, mine_ref,
-    den, bra, ket, t_ref, u_ref, mom, part, sib, lists, c_leaf, c_top, x_ref, v_high, v_low, v_top,
-    leaf_out, top_out, leaf_in, top_in, dom, rows_ref, acc, kids,
-    load_sem, table_sem, list_send, list_recv, sib_send, sib_recv,
+    den_hbm, bra_hbm, ket_hbm, box_hbm, lsrc_hbm, ltype_hbm, csrc_hbm, ctype_hbm, t_hbm, u_hbm,
+    bra, ket, rows_ref, mine_ref,
+    box_ref, lsrc_ref, ltype_ref, csrc_ref, ctype_ref, den, t_ref, u_ref, mom, part, sib, lists, c_leaf, c_top, x_ref, v_high, v_low, v_top,
+    leaf_out, top_out, leaf_in, top_in, dom, acc, kids,
+    small_sem, load_sem, table_sem, list_send, list_recv, sib_send, sib_recv,
     leaf_send, leaf_recv, top_send, top_recv, dom_send, dom_recv,
 ):
     s = lax.axis_index("space")
@@ -75,14 +67,18 @@
     me = s * nz + z
     groups = n_space * nz
 
-    barrier = pltpu.get_barrier_semaphore()
-    for o in range(1, groups):
-        g = lax.rem(me + o, groups)
-        pl.semaphore_signal(
-            barrier, inc=1, device_id=(g // nz, lax.rem(g, nz) * 2 + core), device_id_type=MESH
-        )
-    for k in range(nz):
-        pl.semaphore_signal(barrier, inc=1, device_id=(s, k * 2 + 1 - core), device_id_type=MESH)
+    small = [
+        pltpu.make_async_copy(src, dst, small_sem.at[k])
+        for k, (src, dst) in enumerate(
+            (
+                (ltype_hbm, ltype_ref),
+                (lsrc_hbm, lsrc_ref),
+                (ctype_hbm, ctype_ref),
+                (csrc_hbm, csrc_ref),
+                (box_hbm, box_ref),
+            )
+        )
+    ]
 
     def loads(i):
         at = pl.ds(i * GROUP, GROUP)
@@ -96,12 +92,40 @@
             copy.start()
         return carry
 
-    lax.fori_loop(0, chunks, start_loads, 0)
+    start_loads(0, 0)
+    for copy in small:
+        copy.start()
+
+    barrier = pltpu.get_barrier_semaphore()
+    for o in range(1, groups):
+        g = lax.rem(me + o, groups)
+        pl.semaphore_signal(
+            barrier, inc=1, device_id=(g // nz, lax.rem(g, nz) * 2 + core), device_id_type=MESH
+        )
+    for k in range(nz):
+        pl.semaphore_signal(barrier, inc=1, device_id=(s, k * 2 + 1 - core), device_id_type=MESH)
+
+    lax.fori_loop(1, chunks, start_loads, 0)
     u_copy = pltpu.make_async_copy(u_hbm, u_ref, table_sem.at[0])
     t_copy = pltpu.make_async_copy(t_hbm, t_ref, table_sem.at[1])
     u_copy.start()
     t_copy.start()
 
+    def moments(i, carry):
+        for copy in loads(i):
+            copy.wait()
+        rows = []
+        for u in range(GROUP):
+            b = i * GROUP + u
+            inner = dot(den[b], ket[b], NN)
+            rows.append(jnp.sum(inner * bra[b].astype(F32), axis=0, keepdims=True))
+        mom[pl.ds(i * GROUP, GROUP), :] = jnp.concatenate(rows, axis=0)
+        return carry
+
+    lax.fori_loop(0, chunks // 2, moments, 0)
+
+    for copy in small:
+        copy.wait()
     lists[pl.ds(me * 16, 8), 0:entries] = ltype_ref[...] * KEY + lsrc_ref[...]
     lists[pl.ds(me * 16 + 8, 1), 0:entries] = ctype_ref[...] * KEY + csrc_ref[...]
     pl.semaphore_wait(barrier, groups - 1 + nz)
@@ -133,18 +157,7 @@
     for o in range(1, groups):
         list_copy(o).start()
 
-    def moments(i, carry):
-        for copy in loads(i):
-            copy.wait()
-        rows = []
-        for u in range(GROUP):
-            b = i * GROUP + u
-            inner = dot(den[b], ket[b], NN)
-            rows.append(jnp.sum(inner * bra[b].astype(F32), axis=0, keepdims=True))
-        mom[pl.ds(i * GROUP, GROUP), :] = jnp.concatenate(rows, axis=0)
-        return carry
-
-    lax.fori_loop(0, chunks, moments, 0)
+    lax.fori_loop(chunks // 2, chunks, moments, 0)
     hot = jnp.where(
         lax.broadcasted_iota(jnp.int32, (box_dom, n_blocks), 0) == box_ref[...], 1.0, 0.0
     ).astype(BF16)
@@ -300,20 +313,6 @@
 
     for o in range(1, n_blk):
         dom_copy(o, j).start()
-    for o in range(1, n_blk):
-        dom_copy(o, lax.rem(j + o, n_blk)).wait_recv()
-
-    rows_ref[...] = one_hot_dot(hot, dom[...], TN)
-
-    def contract(i, carry):
-        local = rows_ref[pl.ds(i * GROUP, GROUP), :]
-        for u in range(GROUP):
-            b = i * GROUP + u
-            scaled = (bra[b].astype(F32) * local[u : u + 1, :]).astype(BF16)
-            out_ref[b] = dot(scaled, ket[b], NT).astype(BF16)
-        return carry
-
-    lax.fori_loop(0, chunks, contract, 0)
 
     for o in range(1, groups):
         list_copy(o).wait_send()
@@ -325,8 +324,36 @@
                 leaf_copy(w, o, (2 - w) * nz + z).wait_send()
     for o in range(1, nz):
         leaf_copy(1, o, nz + z).wait_send()
+
+    for o in range(1, n_blk):
+        dom_copy(o, lax.rem(j + o, n_blk)).wait_recv()
+    rows_ref[...] = one_hot_dot(hot, dom[...], TN)
     for o in range(1, n_blk):
         dom_copy(o, j).wait_send()
+
+
+def contract(bra, ket, rows_ref, mine_ref, out_hbm, mine_hbm, out, out_sem, mine_sem):
+    chunks = bra.shape[0] // GROUP
+    mine_copy = pltpu.make_async_copy(mine_ref, mine_hbm, mine_sem)
+    mine_copy.start()
+
+    def store(i):
+        at = pl.ds(i * GROUP, GROUP)
+        return pltpu.make_async_copy(out.at[at], out_hbm.at[at], out_sem.at[i])
+
+    def step(i, carry):
+        local = rows_ref[pl.ds(i * GROUP, GROUP), :]
+        for u in range(GROUP):
+            b = i * GROUP + u
+            scaled = (bra[b].astype(F32) * local[u : u + 1, :]).astype(BF16)
+            out[b] = dot(scaled, ket[b], NT).astype(BF16)
+        store(i).start()
+        return carry
+
+    lax.fori_loop(0, chunks, step, 0)
+    for i in range(chunks):
+        store(i).wait()
+    mine_copy.wait()
 
 
 def shards(
@@ -352,20 +379,26 @@
     chunks = n_blocks // GROUP
     x_rows = -(-(box_dom + top_dom) // 16) * 16
     whole = pl.BlockSpec(memory_space=pltpu.VMEM)
-    far = pl.BlockSpec(memory_space=pl.ANY)
+    far = pl.BlockSpec(memory_space=pltpu.HBM)
     dma = pltpu.SemaphoreType.DMA
-    coulomb, box_locals = pl.pallas_call(
+    ints = jnp.int32
+    bra_here, ket_here, rows, mine = pl.pallas_call(
         functools.partial(build, n_space, n_blk, n_types),
         out_shape=(
-            jax.ShapeDtypeStruct((n_blocks, side, side), BF16),
+            jax.ShapeDtypeStruct(bra_table.shape, BF16),
+            jax.ShapeDtypeStruct(ket_table.shape, BF16),
+            jax.ShapeDtypeStruct((n_blocks, coeffs), F32),
             jax.ShapeDtypeStruct((8, coeffs), F32),
         ),
-        in_specs=[far, far, far, whole, whole, whole, whole, whole, far, far],
-        out_specs=(whole, whole),
+        in_specs=[far] * 10,
+        out_specs=(whole,) * 4,
         scratch_shapes=[
+            pltpu.VMEM((1, n_blocks), ints),
+            pltpu.VMEM(leaf_src.shape, ints),
+            pltpu.VMEM(leaf_type.shape, ints),
+            pltpu.VMEM(coarse_src.shape, ints),
+            pltpu.VMEM(coarse_type.shape, ints),
             pltpu.VMEM(density.shape, BF16),
-            pltpu.VMEM(bra_table.shape, BF16),
-            pltpu.VMEM(ket_table.shape, BF16),
             pltpu.VMEM(translation.shape, F32),
             pltpu.VMEM(upward_translation_table.shape, F32),
             pltpu.VMEM((n_blocks, coeffs), F32),
@@ -383,9 +416,9 @@
             pltpu.VMEM((3 * nz, 8, coeffs), F32),
             pltpu.VMEM((groups, 1, coeffs), F32),
             pltpu.VMEM((box_dom, coeffs), F32),
-            pltpu.VMEM((n_blocks, coeffs), F32),
             pltpu.VMEM((8, coeffs), F32),
             pltpu.VMEM((2 * box_dom, coeffs // 2), F32),
+            dma((5,)),
             dma((3, chunks)),
             dma((2,)),
             dma((groups,)),
@@ -400,26 +433,50 @@
             dma((n_blk,)),
         ],
         compiler_params=pltpu.CompilerParams(
-            collective_id=0, has_side_effects=True, vmem_limit_bytes=48 * 1024 * 1024
+            collective_id=0, has_side_effects=True, vmem_limit_bytes=28 * 1024 * 1024
         ),
         cost_estimate=pl.CostEstimate(
-            flops=4 * n_blocks * side * side * coeffs,
-            bytes_accessed=30_000_000,
+            flops=2 * n_blocks * side * side * coeffs,
+            bytes_accessed=22_000_000,
             transcendentals=0,
         ),
     )(
-        density,
-        bra_table,
-        ket_table,
-        box_of_block[None, :],
-        leaf_src,
-        leaf_type,
-        coarse_src,
-        coarse_type,
-        translation,
-        upward_translation_table,
+        *(
+            pltpu.with_memory_space_constraint(x, pltpu.HBM)
+            for x in (
+                density,
+                bra_table,
+                ket_table,
+                box_of_block[None, :],
+                leaf_src,
+                leaf_type,
+                coarse_src,
+                coarse_type,
+                translation,
+                upward_translation_table,
+            )
+        )
     )
-    return coulomb, box_locals
+    return pl.pallas_call(
+        contract,
+        out_shape=(
+            jax.ShapeDtypeStruct((n_blocks, side, side), BF16),
+            jax.ShapeDtypeStruct((8, coeffs), F32),
+        ),
+        in_specs=[whole] * 4,
+        out_specs=(far, far),
+        scratch_shapes=[
+            pltpu.VMEM((n_blocks, side, side), BF16),
+            dma((chunks,)),
+            dma,
+        ],
+        compiler_params=pltpu.CompilerParams(vmem_limit_bytes=16 * 1024 * 1024),
+        cost_estimate=pl.CostEstimate(
+            flops=2 * n_blocks * side * side * coeffs,
+            bytes_accessed=2 * n_blocks * side * side,
+            transcendentals=0,
+        ),
+    )(bra_here, ket_here, rows, mine)
 
 
 def solution(mesh):

time: 36.8 us -> 31.4 us (0.85)
  local copies, waits for them, and re-layouts: 7.19 us -> 0 us
  Pallas kernels: 28.7 us -> 30.6 us
    unnamed x14 -> x0, local copies, waits for them, and re-layouts: 7.19 us -> none
    pallas_call x0 -> x1, Pallas kernels: none -> 4.51 us  [shards(): pl.pallas_call(contract, out_shape=(jax.ShapeDtypeStruct((n_blocks, side,...]
    pallas_call x1, Pallas kernels: 28.7 us -> 26.1 us  [shards(): pl.pallas_call(functools.partial(build, n_space, n_blk, n_types), out_sha...]
where the time goes in v2:
time: 31.4 us; the launch traced here: 31.2 us
  Pallas kernels  30.6 us (97%)
  between operations  0.64 us (2%)
    pallas_call x1, Pallas kernels, shards(): pl.pallas_call(functools.partial(build, n_space, n_blk, n_types), out_sha...  26.1 us
    pallas_call x1, Pallas kernels, shards(): pl.pallas_call(contract, out_shape=(jax.ShapeDtypeStruct((n_blocks, side,...  4.51 us

profile of v2, /device:TPU:0, one launch (start us, length us, event | category | flops | bytes accessed | tf_op | source)
XLA Modules:
  0.0 31.2 jit_solution(5468568833413006036)
XLA Ops:
  0.6 26.1 %shard_map.113 = (bf16[96,128,256]{2,1,0:T(8,128)(2,1)S(1)}, bf16[96,128,256]{2,1,0:T(8,128)(2,1)S(1)}, f32[96,256]{1,0:T(8,128)S(1)}, f32[8,256]{1,0:T(8,128)S(1)}) custom-call(bf16[96,128,128]{2,1,0:T(8,128)(2,1)} %den_hbm.1, bf16[96,128,256]{2,1,0:T(8,128)(2,1)} %bra_hbm.1, bf16[96,128,256]{2,1,0:T(8,128)(2,1)} %ket_hbm.1, s32[1,96]{1,0:T(1,128)} %bitcast.1, ...), custom_call_target="tpu_custom_call" | custom-call | flops 805306368 | bytes 22000000 | tf_op jit(solution)/shard_map/pallas_call | solution.py:385
  26.7 4.5 %shard_map.114 = (bf16[96,128,128]{2,1,0:T(8,128)(2,1)}, f32[8,256]{1,0:T(8,128)}) custom-call(bf16[96,128,256]{2,1,0:T(8,128)(2,1)S(1)} %get-tuple-element.6.bra, bf16[96,128,256]{2,1,0:T(8,128)(2,1)S(1)} %get-tuple-element.7.ket, f32[96,256]{1,0:T(8,128)S(1)} %get-tuple-element.8.rows_ref, f32[8,256]{1,0:T(8,128)S(1)} %get-tuple-element.9.mine_ref), custom_call_target="tpu_custom_call" | custom-call | flops 805306368 | bytes 3145728 | tf_op jit(solution)/shard_map/pallas_call | solution.py:460

commit v3 on v2

--- a/solution.py
+++ b/solution.py
@@ -10,7 +10,8 @@
 MESH = pl.DeviceIdType.MESH
 F32 = jnp.float32
 BF16 = jnp.bfloat16
-GROUP = 8
+GROUP = 16
+UNROLL = 4
 KEY = 1024
 
 
@@ -108,8 +109,6 @@
     lax.fori_loop(1, chunks, start_loads, 0)
     u_copy = pltpu.make_async_copy(u_hbm, u_ref, table_sem.at[0])
     t_copy = pltpu.make_async_copy(t_hbm, t_ref, table_sem.at[1])
-    u_copy.start()
-    t_copy.start()
 
     def moments(i, carry):
         for copy in loads(i):
@@ -123,6 +122,8 @@
         return carry
 
     lax.fori_loop(0, chunks // 2, moments, 0)
+    u_copy.start()
+    t_copy.start()
 
     for copy in small:
         copy.wait()
@@ -175,15 +176,17 @@
 
     for o in range(1, groups):
         list_arrival(o).wait_recv()
-    for w in range(3):
-        sender_at = 2 - w
-        target = jnp.clip(s + w - 1, 0, n_space - 1)
-        for k in range(nz):
-            packed = lists[pl.ds((target * nz + k) * 16, 8), 0:entries]
-            kind = lax.shift_right_logical(packed, 10)
-            place = (packed & (KEY - 1)) - sender_at * box_dom
-            keys = jnp.where((place >= 0) & (place < box_dom), kind * box_dom + place, -1)
-            c_leaf[pl.ds((w * nz + k) * 8, 8), :] = count_hot(keys, n_types * box_dom)
+    def counts(n, carry):
+        w = n // nz
+        target = jnp.clip(s + w - 1, 0, n_space - 1) * nz + lax.rem(n, nz)
+        packed = lists[pl.ds(pl.multiple_of(target * 16, 16), 8), 0:entries]
+        kind = lax.shift_right_logical(packed, 10)
+        place = (packed & (KEY - 1)) - (2 - w) * box_dom
+        keys = jnp.where((place >= 0) & (place < box_dom), kind * box_dom + place, -1)
+        c_leaf[pl.ds(pl.multiple_of(n * 8, 8), 8), :] = count_hot(keys, n_types * box_dom)
+        return carry
+
+    lax.fori_loop(0, 3 * nz, counts, 0)
     packed = lists[pl.ds(8, groups, stride=16), :]
     kind = lax.shift_right_logical(packed, 10)
     place = (packed & (KEY - 1)) - s * top_dom
@@ -216,14 +219,20 @@
     x_high, x_low = halves(x)
     x_rows = x.shape[0]
     stack = jnp.concatenate([x_high, x_low], axis=0)
-    for t in range(n_types):
-        t_high, t_low = halves(t_ref[t])
-        both = dot(stack, t_high, NT)
-        v = both[:x_rows] + both[x_rows:] + dot(x_high, t_low, NT)
-        high, low = halves(v[:box_dom])
-        v_high[t * box_dom : (t + 1) * box_dom, :] = high
-        v_low[t * box_dom : (t + 1) * box_dom, :] = low
-        v_top[t * top_dom : (t + 1) * top_dom, :] = v[box_dom : box_dom + top_dom]
+    def translate(i, carry):
+        for u in range(UNROLL):
+            t = i * UNROLL + u
+            t_high, t_low = halves(t_ref[t])
+            both = dot(stack, t_high, NT)
+            v = both[:x_rows] + both[x_rows:] + dot(x_high, t_low, NT)
+            high, low = halves(v[:box_dom])
+            at = pl.ds(pl.multiple_of(t * box_dom, 16), box_dom)
+            v_high[at, :] = high
+            v_low[at, :] = low
+            v_top[pl.ds(pl.multiple_of(t * top_dom, 8), top_dom), :] = v[box_dom : box_dom + top_dom]
+        return carry
+
+    lax.fori_loop(0, n_types // UNROLL, translate, 0)
 
     sent_top = one_hot_dot(c_top[...].astype(BF16), v_top[...], NN)
     for g in range(groups):
@@ -343,10 +352,14 @@
 
     def step(i, carry):
         local = rows_ref[pl.ds(i * GROUP, GROUP), :]
-        for u in range(GROUP):
-            b = i * GROUP + u
-            scaled = (bra[b].astype(F32) * local[u : u + 1, :]).astype(BF16)
-            out[b] = dot(scaled, ket[b], NT).astype(BF16)
+        for first in range(0, GROUP, UNROLL):
+            made = []
+            for u in range(first, first + UNROLL):
+                b = i * GROUP + u
+                scaled = (bra[b].astype(F32) * local[u : u + 1, :]).astype(BF16)
+                made.append(dot(scaled, ket[b], NT).astype(BF16))
+            for u in range(UNROLL):
+                out[i * GROUP + first + u] = made[u]
         store(i).start()
         return carry
 

time: 31.4 us -> 31.7 us (level)
    pallas_call x1, Pallas kernels: 26.1 us -> 27.3 us  [shards(): pl.pallas_call(functools.partial(build, n_space, n_blk, n_types), out_sha...]
    pallas_call x1, Pallas kernels: 4.51 us -> 3.56 us  [shards(): pl.pallas_call(contract, out_shape=(jax.ShapeDtypeStruct((n_blocks, side,...]
where the time goes in v3:
time: 31.7 us; the launch traced here: 31.5 us
  Pallas kernels  30.9 us (97%)
  between operations  0.64 us (2%)
    pallas_call x1, Pallas kernels, shards(): pl.pallas_call(functools.partial(build, n_space, n_blk, n_types), out_sha...  27.3 us
    pallas_call x1, Pallas kernels, shards(): pl.pallas_call(contract, out_shape=(jax.ShapeDtypeStruct((n_blocks, side,...  3.56 us

profile of v3, /device:TPU:0, one launch (start us, length us, event | category | flops | bytes accessed | tf_op | source)
XLA Modules:
  0.0 31.5 jit_solution(15212665264211160800)
XLA Ops:
  0.6 27.3 %shard_map.113 = (bf16[96,128,256]{2,1,0:T(8,128)(2,1)S(1)}, bf16[96,128,256]{2,1,0:T(8,128)(2,1)S(1)}, f32[96,256]{1,0:T(8,128)S(1)}, f32[8,256]{1,0:T(8,128)S(1)}) custom-call(bf16[96,128,128]{2,1,0:T(8,128)(2,1)} %den_hbm.1, bf16[96,128,256]{2,1,0:T(8,128)(2,1)} %bra_hbm.1, bf16[96,128,256]{2,1,0:T(8,128)(2,1)} %ket_hbm.1, s32[1,96]{1,0:T(1,128)} %bitcast.1, ...), custom_call_target="tpu_custom_call" | custom-call | flops 805306368 | bytes 22000000 | tf_op jit(solution)/shard_map/pallas_call | solution.py:398
  28.0 3.6 %shard_map.114 = (bf16[96,128,128]{2,1,0:T(8,128)(2,1)}, f32[8,256]{1,0:T(8,128)}) custom-call(bf16[96,128,256]{2,1,0:T(8,128)(2,1)S(1)} %get-tuple-element.6.bra, bf16[96,128,256]{2,1,0:T(8,128)(2,1)S(1)} %get-tuple-element.7.ket, f32[96,256]{1,0:T(8,128)S(1)} %get-tuple-element.8.rows_ref, f32[8,256]{1,0:T(8,128)S(1)} %get-tuple-element.9.mine_ref), custom_call_target="tpu_custom_call" | custom-call | flops 805306368 | bytes 3145728 | tf_op jit(solution)/shard_map/pallas_call | solution.py:473

commit v4 on v3

--- a/solution.py
+++ b/solution.py
@@ -49,7 +49,8 @@
     n_types,
     den_hbm, bra_hbm, ket_hbm, box_hbm, lsrc_hbm, ltype_hbm, csrc_hbm, ctype_hbm, t_hbm, u_hbm,
     bra, ket, rows_ref, mine_ref,
-    box_ref, lsrc_ref, ltype_ref, csrc_ref, ctype_ref, den, t_ref, u_ref, mom, part, sib, lists, c_leaf, c_top, x_ref, v_high, v_low, v_top,
+    box_ref, lsrc_ref, ltype_ref, csrc_ref, ctype_ref, den, t_ref, u_ref,
+    t_high, t_low, u_high, u_low, mom, part, sib, lists, c_leaf, c_top, x_ref, v_high, v_low, v_top,
     leaf_out, top_out, leaf_in, top_in, dom, acc, kids,
     small_sem, load_sem, table_sem, list_send, list_recv, sib_send, sib_recv,
     leaf_send, leaf_recv, top_send, top_recv, dom_send, dom_recv,
@@ -110,7 +111,7 @@
     u_copy = pltpu.make_async_copy(u_hbm, u_ref, table_sem.at[0])
     t_copy = pltpu.make_async_copy(t_hbm, t_ref, table_sem.at[1])
 
-    def moments(i, carry):
+    def moments(i):
         for copy in loads(i):
             copy.wait()
         rows = []
@@ -119,9 +120,30 @@
             inner = dot(den[b], ket[b], NN)
             rows.append(jnp.sum(inner * bra[b].astype(F32), axis=0, keepdims=True))
         mom[pl.ds(i * GROUP, GROUP), :] = jnp.concatenate(rows, axis=0)
+
+    def counts(n):
+        w = n // nz
+        target = jnp.clip(s + w - 1, 0, n_space - 1) * nz + lax.rem(n, nz)
+        packed = lists[pl.ds(pl.multiple_of(target * 16, 16), 8), 0:entries]
+        kind = lax.shift_right_logical(packed, 10)
+        place = (packed & (KEY - 1)) - (2 - w) * box_dom
+        keys = jnp.where((place >= 0) & (place < box_dom), kind * box_dom + place, -1)
+        c_leaf[pl.ds(pl.multiple_of(n * 8, 8), 8), :] = count_hot(keys, n_types * box_dom)
+
+    early = chunks // 2
+    each = 3 * nz // (chunks - early)
+
+    def moments_alone(i, carry):
+        moments(i)
         return carry
 
-    lax.fori_loop(0, chunks // 2, moments, 0)
+    def moments_and_counts(i, carry):
+        moments(i)
+        for k in range(each):
+            counts((i - early) * each + k)
+        return carry
+
+    lax.fori_loop(0, 1, moments_alone, 0)
     u_copy.start()
     t_copy.start()
 
@@ -158,7 +180,10 @@
     for o in range(1, groups):
         list_copy(o).start()
 
-    lax.fori_loop(chunks // 2, chunks, moments, 0)
+    lax.fori_loop(1, early, moments_alone, 0)
+    for o in range(1, groups):
+        list_arrival(o).wait_recv()
+    lax.fori_loop(early, chunks, moments_and_counts, 0)
     hot = jnp.where(
         lax.broadcasted_iota(jnp.int32, (box_dom, n_blocks), 0) == box_ref[...], 1.0, 0.0
     ).astype(BF16)
@@ -174,19 +199,6 @@
     )
     sib_copy.start()
 
-    for o in range(1, groups):
-        list_arrival(o).wait_recv()
-    def counts(n, carry):
-        w = n // nz
-        target = jnp.clip(s + w - 1, 0, n_space - 1) * nz + lax.rem(n, nz)
-        packed = lists[pl.ds(pl.multiple_of(target * 16, 16), 8), 0:entries]
-        kind = lax.shift_right_logical(packed, 10)
-        place = (packed & (KEY - 1)) - (2 - w) * box_dom
-        keys = jnp.where((place >= 0) & (place < box_dom), kind * box_dom + place, -1)
-        c_leaf[pl.ds(pl.multiple_of(n * 8, 8), 8), :] = count_hot(keys, n_types * box_dom)
-        return carry
-
-    lax.fori_loop(0, 3 * nz, counts, 0)
     packed = lists[pl.ds(8, groups, stride=16), :]
     kind = lax.shift_right_logical(packed, 10)
     place = (packed & (KEY - 1)) - s * top_dom
@@ -195,6 +207,21 @@
 
     u_copy.wait()
     t_copy.wait()
+
+    def split_table(i, carry):
+        high, low = halves(t_ref[i])
+        t_high[i] = high
+        t_low[i] = low
+
+        @pl.when(i < 8)
+        def _():
+            high, low = halves(u_ref[i])
+            u_high[i] = high
+            u_low[i] = low
+
+        return carry
+
+    lax.fori_loop(0, n_types, split_table, 0)
     sib_copy.wait()
     own = part[...] + sib[...]
     x_ref[0:box_dom, :] = own
@@ -209,9 +236,8 @@
         )
         c_high, c_low = halves(child)
         stack = jnp.concatenate([c_high.astype(F32), c_low.astype(F32)], axis=0).astype(BF16)
-        u_high, u_low = halves(u_ref[c])
-        both = dot(stack, u_high, NT)
-        extra = dot(stack, u_low, NT)
+        both = dot(stack, u_high[c], NT)
+        extra = dot(stack, u_low[c], NT)
         tops += both[:top_dom] + both[top_dom:] + extra[:top_dom]
     x_ref[box_dom : box_dom + top_dom, :] = tops
 
@@ -219,20 +245,13 @@
     x_high, x_low = halves(x)
     x_rows = x.shape[0]
     stack = jnp.concatenate([x_high, x_low], axis=0)
-    def translate(i, carry):
-        for u in range(UNROLL):
-            t = i * UNROLL + u
-            t_high, t_low = halves(t_ref[t])
-            both = dot(stack, t_high, NT)
-            v = both[:x_rows] + both[x_rows:] + dot(x_high, t_low, NT)
-            high, low = halves(v[:box_dom])
-            at = pl.ds(pl.multiple_of(t * box_dom, 16), box_dom)
-            v_high[at, :] = high
-            v_low[at, :] = low
-            v_top[pl.ds(pl.multiple_of(t * top_dom, 8), top_dom), :] = v[box_dom : box_dom + top_dom]
-        return carry
-
-    lax.fori_loop(0, n_types // UNROLL, translate, 0)
+    for t in range(n_types):
+        both = dot(stack, t_high[t], NT)
+        v = both[:x_rows] + both[x_rows:] + dot(x_high, t_low[t], NT)
+        high, low = halves(v[:box_dom])
+        v_high[t * box_dom : (t + 1) * box_dom, :] = high
+        v_low[t * box_dom : (t + 1) * box_dom, :] = low
+        v_top[t * top_dom : (t + 1) * top_dom, :] = v[box_dom : box_dom + top_dom]
 
     sent_top = one_hot_dot(c_top[...].astype(BF16), v_top[...], NN)
     for g in range(groups):
@@ -289,9 +308,8 @@
     ).astype(BF16)
     down = []
     for c in range(8):
-        u_high, u_low = halves(u_ref[c])
-        both = dot(stack, u_high, NN)
-        extra = dot(stack, u_low, NN)
+        both = dot(stack, u_high[c], NN)
+        extra = dot(stack, u_low[c], NN)
         down.append(both[0:1] + both[1:2] + extra[0:1])
     acc[...] = jnp.concatenate(down, axis=0) + leaf_out[pl.ds(nz + z, 1)][0]
     for o in range(1, nz):
@@ -414,6 +432,10 @@
             pltpu.VMEM(density.shape, BF16),
             pltpu.VMEM(translation.shape, F32),
             pltpu.VMEM(upward_translation_table.shape, F32),
+            pltpu.VMEM(translation.shape, BF16),
+            pltpu.VMEM(translation.shape, BF16),
+            pltpu.VMEM(upward_translation_table.shape, BF16),
+            pltpu.VMEM(upward_translation_table.shape, BF16),
             pltpu.VMEM((n_blocks, coeffs), F32),
             pltpu.VMEM((box_dom, coeffs), F32),
             pltpu.VMEM((box_dom, coeffs), F32),
@@ -446,7 +468,7 @@
             dma((n_blk,)),
         ],
         compiler_params=pltpu.CompilerParams(
-            collective_id=0, has_side_effects=True, vmem_limit_bytes=28 * 1024 * 1024
+            collective_id=0, has_side_effects=True, vmem_limit_bytes=32 * 1024 * 1024
         ),
         cost_estimate=pl.CostEstimate(
             flops=2 * n_blocks * side * side * coeffs,

time: 31.7 us -> 31.9 us (level)
  no operation moved by 1% of the time
where the time goes in v4:
time: 31.9 us; the launch traced here: 31.7 us
  Pallas kernels  31.1 us (97%)
  between operations  0.64 us (2%)
    pallas_call x1, Pallas kernels, shards(): pl.pallas_call(functools.partial(build, n_space, n_blk, n_types), out_sha...  27.6 us
    pallas_call x1, Pallas kernels, shards(): pl.pallas_call(contract, out_shape=(jax.ShapeDtypeStruct((n_blocks, side,...  3.54 us

profile of v4, /device:TPU:0, one launch (start us, length us, event | category | flops | bytes accessed | tf_op | source)
XLA Modules:
  0.0 31.7 jit_solution(12417005908447002982)
XLA Ops:
  0.6 27.6 %shard_map.113 = (bf16[96,128,256]{2,1,0:T(8,128)(2,1)S(1)}, bf16[96,128,256]{2,1,0:T(8,128)(2,1)S(1)}, f32[96,256]{1,0:T(8,128)S(1)}, f32[8,256]{1,0:T(8,128)S(1)}) custom-call(bf16[96,128,128]{2,1,0:T(8,128)(2,1)} %den_hbm.1, bf16[96,128,256]{2,1,0:T(8,128)(2,1)} %bra_hbm.1, bf16[96,128,256]{2,1,0:T(8,128)(2,1)} %ket_hbm.1, s32[1,96]{1,0:T(1,128)} %bitcast.1, ...), custom_call_target="tpu_custom_call" | custom-call | flops 805306368 | bytes 22000000 | tf_op jit(solution)/shard_map/pallas_call | solution.py:416
  28.2 3.5 %shard_map.114 = (bf16[96,128,128]{2,1,0:T(8,128)(2,1)}, f32[8,256]{1,0:T(8,128)}) custom-call(bf16[96,128,256]{2,1,0:T(8,128)(2,1)S(1)} %get-tuple-element.6.bra, bf16[96,128,256]{2,1,0:T(8,128)(2,1)S(1)} %get-tuple-element.7.ket, f32[96,256]{1,0:T(8,128)S(1)} %get-tuple-element.8.rows_ref, f32[8,256]{1,0:T(8,128)S(1)} %get-tuple-element.9.mine_ref), custom_call_target="tpu_custom_call" | custom-call | flops 805306368 | bytes 3145728 | tf_op jit(solution)/shard_map/pallas_call | solution.py:495

commit v5 on v2

--- a/solution.py
+++ b/solution.py
@@ -11,6 +11,8 @@
 F32 = jnp.float32
 BF16 = jnp.bfloat16
 GROUP = 8
+STEP = 16
+PIECES = 4
 KEY = 1024
 
 
@@ -107,9 +109,13 @@
 
     lax.fori_loop(1, chunks, start_loads, 0)
     u_copy = pltpu.make_async_copy(u_hbm, u_ref, table_sem.at[0])
-    t_copy = pltpu.make_async_copy(t_hbm, t_ref, table_sem.at[1])
     u_copy.start()
-    t_copy.start()
+    piece = n_types // PIECES
+    t_copies = []
+    for i in range(PIECES):
+        at = pl.ds(i * piece, piece)
+        t_copies.append(pltpu.make_async_copy(t_hbm.at[at], t_ref.at[at], table_sem.at[1 + i]))
+        t_copies[i].start()
 
     def moments(i, carry):
         for copy in loads(i):
@@ -191,7 +197,6 @@
     c_top[...] = count_hot(keys[:, 0:entries], n_types * top_dom)
 
     u_copy.wait()
-    t_copy.wait()
     sib_copy.wait()
     own = part[...] + sib[...]
     x_ref[0:box_dom, :] = own
@@ -217,6 +222,8 @@
     x_rows = x.shape[0]
     stack = jnp.concatenate([x_high, x_low], axis=0)
     for t in range(n_types):
+        if t % piece == 0:
+            t_copies[t // piece].wait()
         t_high, t_low = halves(t_ref[t])
         both = dot(stack, t_high, NT)
         v = both[:x_rows] + both[x_rows:] + dot(x_high, t_low, NT)
@@ -333,25 +340,29 @@
 
 
 def contract(bra, ket, rows_ref, mine_ref, out_hbm, mine_hbm, out, out_sem, mine_sem):
-    chunks = bra.shape[0] // GROUP
     mine_copy = pltpu.make_async_copy(mine_ref, mine_hbm, mine_sem)
     mine_copy.start()
 
     def store(i):
-        at = pl.ds(i * GROUP, GROUP)
+        at = pl.ds(i * STEP, STEP)
         return pltpu.make_async_copy(out.at[at], out_hbm.at[at], out_sem.at[i])
 
     def step(i, carry):
-        local = rows_ref[pl.ds(i * GROUP, GROUP), :]
-        for u in range(GROUP):
-            b = i * GROUP + u
-            scaled = (bra[b].astype(F32) * local[u : u + 1, :]).astype(BF16)
-            out[b] = dot(scaled, ket[b], NT).astype(BF16)
+        local = rows_ref[pl.ds(i * STEP, STEP), :]
+        for first in range(0, STEP, 4):
+            made = []
+            for u in range(first, first + 4):
+                b = i * STEP + u
+                scaled = (bra[b].astype(F32) * local[u : u + 1, :]).astype(BF16)
+                made.append(dot(scaled, ket[b], NT).astype(BF16))
+            for u in range(4):
+                out[i * STEP + first + u] = made[u]
         store(i).start()
         return carry
 
-    lax.fori_loop(0, chunks, step, 0)
-    for i in range(chunks):
+    steps = bra.shape[0] // STEP
+    lax.fori_loop(0, steps, step, 0)
+    for i in range(steps):
         store(i).wait()
     mine_copy.wait()
 
@@ -420,7 +431,7 @@
             pltpu.VMEM((2 * box_dom, coeffs // 2), F32),
             dma((5,)),
             dma((3, chunks)),
-            dma((2,)),
+            dma((1 + PIECES,)),
             dma((groups,)),
             dma((groups,)),
             dma,
@@ -467,7 +478,7 @@
         out_specs=(far, far),
         scratch_shapes=[
             pltpu.VMEM((n_blocks, side, side), BF16),
-            dma((chunks,)),
+            dma((n_blocks // STEP,)),
             dma,
         ],
         compiler_params=pltpu.CompilerParams(vmem_limit_bytes=16 * 1024 * 1024),

time: 31.4 us -> 30.9 us (0.984)
  Pallas kernels: 30.6 us -> 30.1 us
    pallas_call x1, Pallas kernels: 4.51 us -> 3.56 us  [shards(): pl.pallas_call(contract, out_shape=(jax.ShapeDtypeStruct((n_blocks, side,...]
    pallas_call x1, Pallas kernels: 26.1 us -> 26.6 us  [shards(): pl.pallas_call(functools.partial(build, n_space, n_blk, n_types), out_sha...]
where the time goes in v5:
time: 30.9 us; the launch traced here: 30.8 us
  Pallas kernels  30.1 us (97%)
  between operations  0.64 us (2%)
    pallas_call x1, Pallas kernels, shards(): pl.pallas_call(functools.partial(build, n_space, n_blk, n_types), out_sha...  26.6 us
    pallas_call x1, Pallas kernels, shards(): pl.pallas_call(contract, out_shape=(jax.ShapeDtypeStruct((n_blocks, side,...  3.56 us

profile of v5, /device:TPU:0, one launch (start us, length us, event | category | flops | bytes accessed | tf_op | source)
XLA Modules:
  0.0 30.8 jit_solution(7406872515078712413)
XLA Ops:
  0.6 26.6 %shard_map.113 = (bf16[96,128,256]{2,1,0:T(8,128)(2,1)S(1)}, bf16[96,128,256]{2,1,0:T(8,128)(2,1)S(1)}, f32[96,256]{1,0:T(8,128)S(1)}, f32[8,256]{1,0:T(8,128)S(1)}) custom-call(bf16[96,128,128]{2,1,0:T(8,128)(2,1)} %den_hbm.1, bf16[96,128,256]{2,1,0:T(8,128)(2,1)} %bra_hbm.1, bf16[96,128,256]{2,1,0:T(8,128)(2,1)} %ket_hbm.1, s32[1,96]{1,0:T(1,128)} %bitcast.1, ...), custom_call_target="tpu_custom_call" | custom-call | flops 805306368 | bytes 22000000 | tf_op jit(solution)/shard_map/pallas_call | solution.py:396
  27.2 3.6 %shard_map.114 = (bf16[96,128,128]{2,1,0:T(8,128)(2,1)}, f32[8,256]{1,0:T(8,128)}) custom-call(bf16[96,128,256]{2,1,0:T(8,128)(2,1)S(1)} %get-tuple-element.6.bra, bf16[96,128,256]{2,1,0:T(8,128)(2,1)S(1)} %get-tuple-element.7.ket, f32[96,256]{1,0:T(8,128)S(1)} %get-tuple-element.8.rows_ref, f32[8,256]{1,0:T(8,128)S(1)} %get-tuple-element.9.mine_ref), custom_call_target="tpu_custom_call" | custom-call | flops 805306368 | bytes 3145728 | tf_op jit(solution)/shard_map/pallas_call | solution.py:471

commit v6 on v5

--- a/solution.py
+++ b/solution.py
@@ -51,7 +51,7 @@
     den_hbm, bra_hbm, ket_hbm, box_hbm, lsrc_hbm, ltype_hbm, csrc_hbm, ctype_hbm, t_hbm, u_hbm,
     bra, ket, rows_ref, mine_ref,
     box_ref, lsrc_ref, ltype_ref, csrc_ref, ctype_ref, den, t_ref, u_ref, mom, part, sib, lists, c_leaf, c_top, x_ref, v_high, v_low, v_top,
-    leaf_out, top_out, leaf_in, top_in, dom, acc, kids,
+    leaf_out, top_out, leaf_in, top_in, dom, acc, kids, hot_rows,
     small_sem, load_sem, table_sem, list_send, list_recv, sib_send, sib_recv,
     leaf_send, leaf_recv, top_send, top_recv, dom_send, dom_recv,
 ):
@@ -128,7 +128,10 @@
         mom[pl.ds(i * GROUP, GROUP), :] = jnp.concatenate(rows, axis=0)
         return carry
 
-    lax.fori_loop(0, chunks // 2, moments, 0)
+    early = chunks // 3
+    turns = max(n for n in range(1, chunks - early + 1) if (groups - 1) % n == 0)
+    each = (groups - 1) // turns
+    lax.fori_loop(0, early, moments, 0)
 
     for copy in small:
         copy.wait()
@@ -160,10 +163,13 @@
             device_id_type=MESH,
         )
 
-    for o in range(1, groups):
-        list_copy(o).start()
-
-    lax.fori_loop(chunks // 2, chunks, moments, 0)
+    def moments_and_lists(i, carry):
+        for k in range(each):
+            list_copy(1 + (i - early) * each + k).start()
+        return moments(i, carry)
+
+    lax.fori_loop(early, early + turns, moments_and_lists, 0)
+    lax.fori_loop(early + turns, chunks, moments, 0)
     hot = jnp.where(
         lax.broadcasted_iota(jnp.int32, (box_dom, n_blocks), 0) == box_ref[...], 1.0, 0.0
     ).astype(BF16)
@@ -178,6 +184,10 @@
         device_id_type=MESH,
     )
     sib_copy.start()
+    same = lax.broadcasted_iota(jnp.int32, (box_dom, box_dom), 0) == lax.broadcasted_iota(
+        jnp.int32, (box_dom, box_dom), 1
+    )
+    hot_rows[...] = dot(hot, jnp.where(same, 1.0, 0.0).astype(BF16), TN)
 
     for o in range(1, groups):
         list_arrival(o).wait_recv()
@@ -334,7 +344,7 @@
 
     for o in range(1, n_blk):
         dom_copy(o, lax.rem(j + o, n_blk)).wait_recv()
-    rows_ref[...] = one_hot_dot(hot, dom[...], TN)
+    rows_ref[...] = one_hot_dot(hot_rows[...].astype(BF16), dom[...], NN)
     for o in range(1, n_blk):
         dom_copy(o, j).wait_send()
 
@@ -429,6 +439,7 @@
             pltpu.VMEM((box_dom, coeffs), F32),
             pltpu.VMEM((8, coeffs), F32),
             pltpu.VMEM((2 * box_dom, coeffs // 2), F32),
+            pltpu.VMEM((n_blocks, box_dom), F32),
             dma((5,)),
             dma((3, chunks)),
             dma((1 + PIECES,)),

time: 30.9 us -> 30.7 us (level)
  no operation moved by 1% of the time
where the time goes in v6:
time: 30.7 us; the launch traced here: 30.5 us
  Pallas kernels  29.9 us (97%)
  between operations  0.64 us (2%)
    pallas_call x1, Pallas kernels, shards(): pl.pallas_call(functools.partial(build, n_space, n_blk, n_types), out_sha...  26.3 us
    pallas_call x1, Pallas kernels, shards(): pl.pallas_call(contract, out_shape=(jax.ShapeDtypeStruct((n_blocks, side,...  3.56 us

profile of v6, /device:TPU:0, one launch (start us, length us, event | category | flops | bytes accessed | tf_op | source)
XLA Modules:
  0.0 30.5 jit_solution(12468441084261351921)
XLA Ops:
  0.6 26.3 %shard_map.113 = (bf16[96,128,256]{2,1,0:T(8,128)(2,1)S(1)}, bf16[96,128,256]{2,1,0:T(8,128)(2,1)S(1)}, f32[96,256]{1,0:T(8,128)S(1)}, f32[8,256]{1,0:T(8,128)S(1)}) custom-call(bf16[96,128,128]{2,1,0:T(8,128)(2,1)} %den_hbm.1, bf16[96,128,256]{2,1,0:T(8,128)(2,1)} %bra_hbm.1, bf16[96,128,256]{2,1,0:T(8,128)(2,1)} %ket_hbm.1, s32[1,96]{1,0:T(1,128)} %bitcast.1, ...), custom_call_target="tpu_custom_call" | custom-call | flops 805306368 | bytes 22000000 | tf_op jit(solution)/shard_map/pallas_call | solution.py:406
  27.0 3.6 %shard_map.114 = (bf16[96,128,128]{2,1,0:T(8,128)(2,1)}, f32[8,256]{1,0:T(8,128)}) custom-call(bf16[96,128,256]{2,1,0:T(8,128)(2,1)S(1)} %get-tuple-element.6.bra, bf16[96,128,256]{2,1,0:T(8,128)(2,1)S(1)} %get-tuple-element.7.ket, f32[96,256]{1,0:T(8,128)S(1)} %get-tuple-element.8.rows_ref, f32[8,256]{1,0:T(8,128)S(1)} %get-tuple-element.9.mine_ref), custom_call_target="tpu_custom_call" | custom-call | flops 805306368 | bytes 3145728 | tf_op jit(solution)/shard_map/pallas_call | solution.py:482

commit v7 on v6

--- a/solution.py
+++ b/solution.py
@@ -10,7 +10,7 @@
 MESH = pl.DeviceIdType.MESH
 F32 = jnp.float32
 BF16 = jnp.bfloat16
-GROUP = 8
+GROUP = 16
 STEP = 16
 PIECES = 4
 KEY = 1024

time: 30.7 us -> 30.8 us (level)
  no operation moved by 1% of the time
where the time goes in v7:
time: 30.8 us; the launch traced here: 30.6 us
  Pallas kernels  30 us (97%)
  between operations  0.64 us (2%)
    pallas_call x1, Pallas kernels, shards(): pl.pallas_call(functools.partial(build, n_space, n_blk, n_types), out_sha...  26.4 us
    pallas_call x1, Pallas kernels, shards(): pl.pallas_call(contract, out_shape=(jax.ShapeDtypeStruct((n_blocks, side,...  3.56 us

profile of v7, /device:TPU:0, one launch (start us, length us, event | category | flops | bytes accessed | tf_op | source)
XLA Modules:
  0.0 30.6 jit_solution(15622569398597859981)
XLA Ops:
  0.6 26.4 %shard_map.113 = (bf16[96,128,256]{2,1,0:T(8,128)(2,1)S(1)}, bf16[96,128,256]{2,1,0:T(8,128)(2,1)S(1)}, f32[96,256]{1,0:T(8,128)S(1)}, f32[8,256]{1,0:T(8,128)S(1)}) custom-call(bf16[96,128,128]{2,1,0:T(8,128)(2,1)} %den_hbm.1, bf16[96,128,256]{2,1,0:T(8,128)(2,1)} %bra_hbm.1, bf16[96,128,256]{2,1,0:T(8,128)(2,1)} %ket_hbm.1, s32[1,96]{1,0:T(1,128)} %bitcast.1, ...), custom_call_target="tpu_custom_call" | custom-call | flops 805306368 | bytes 22000000 | tf_op jit(solution)/shard_map/pallas_call | solution.py:406
  27.1 3.6 %shard_map.114 = (bf16[96,128,128]{2,1,0:T(8,128)(2,1)}, f32[8,256]{1,0:T(8,128)}) custom-call(bf16[96,128,256]{2,1,0:T(8,128)(2,1)S(1)} %get-tuple-element.6.bra, bf16[96,128,256]{2,1,0:T(8,128)(2,1)S(1)} %get-tuple-element.7.ket, f32[96,256]{1,0:T(8,128)S(1)} %get-tuple-element.8.rows_ref, f32[8,256]{1,0:T(8,128)S(1)} %get-tuple-element.9.mine_ref), custom_call_target="tpu_custom_call" | custom-call | flops 805306368 | bytes 3145728 | tf_op jit(solution)/shard_map/pallas_call | solution.py:482
